TPU v7x, 512 devices: a whole 4x4x16 slice. The times are simulated.
512 devices in a mesh: pb: 32 (over x_lo, z), ka: 16 (over y, x_hi, core).
Axes of the slice: x: 4 (x_hi: 2, x_lo: 2; x = x_hi * 2 + x_lo), y: 4, z: 16, core: 2. Of those that a mesh axis runs over, the one named last changes fastest.
Arguments:
- segments: float32 [8192, 1024], P(('pb', 'ka')), may hold values from -0.25 to 0.25
- futures: float32 [8192, 1024], P(('pb', 'ka')), may hold values from -0.25 to 0.25
- pair_index: int32 [8192], P('pb'), may hold values from 0 to 8191, each once
- log_scale: float32 [1], replicated, may hold values from 1.5 to 2.5
- logit_bias: float32 [1], replicated, may hold values from -7 to -5
Outputs:
- grad_segments: float32 [8192, 1024], P(('pb', 'ka'))
- grad_futures: float32 [8192, 1024], P(('pb', 'ka'))
- scalar_values: float32 [3], replicated
Inputs may be any that keep to these rules, and one draw needn't show every extreme that they name: `pair_index`: every key row is the positive of exactly one query row.
All inputs are finite; a program needn't handle non-finite values.
Results may differ from a plain program's by a relative error of at most 0.0003.
Values sent between devices are 32-bit elements; how exact they have to be, the bound alone decides.
A program may use at most 64 MiB of HBM per device.

v0:
```python
import jax
import jax.numpy as jnp
from jax import lax
from jax.sharding import PartitionSpec as P

epsilon = 1e-06


def unit_rows(matrix):
    inverse = lax.rsqrt(jnp.sum(matrix * matrix, axis=1, keepdims=True) + epsilon)
    return (matrix * inverse, inverse)


def backward_norm(direction, grad_dir, inverse):
    return (grad_dir - direction * jnp.sum(direction * grad_dir, axis=1, keepdims=True)) * inverse


def tile_terms(query_block, key_piece, target, scale_value, offset_value):
    logits = (
        scale_value * jnp.dot(query_block, key_piece.T, precision=lax.Precision.HIGHEST)
        + offset_value
    )
    columns = lax.broadcasted_iota(jnp.int32, logits.shape, 1)
    hitmask = columns == target[:, None]
    weights = jax.nn.sigmoid(logits) - hitmask.astype(jnp.float32)
    partial_value = jnp.stack(
        [
            jnp.sum(jax.nn.softplus(logits))
            - jnp.sum(jnp.where(hitmask, logits, jnp.float32(0.0))),
            jnp.sum(weights * (logits - offset_value)),
            jnp.sum(weights),
        ]
    )
    return (weights, partial_value)


def per_device(segments, futures, pair_index, log_scale, logit_bias):
    local_rows = segments.shape[0]
    across_ka = lax.axis_size("ka")
    across_pb = lax.axis_size("pb")
    all_rows = local_rows * across_pb * across_ka
    query_unit, query_inv = unit_rows(segments)
    key_unit, key_inv = unit_rows(futures)
    scale_value = jnp.exp(log_scale[0])
    offset_value = logit_bias[0]
    column_index = lax.axis_index("ka")
    owner = pair_index // local_rows % across_ka
    position = pair_index // (local_rows * across_ka) * local_rows + pair_index % local_rows
    target = jnp.where(owner == column_index, position, -1)
    query_block = lax.all_gather(query_unit, "ka", axis=0, tiled=True)
    key_block = lax.all_gather(key_unit, "pb", axis=0, tiled=True)
    weights, partial_value = tile_terms(query_block, key_block, target, scale_value, offset_value)
    query_terms = scale_value * jnp.dot(weights, key_block, precision=lax.Precision.HIGHEST)
    key_terms = scale_value * jnp.dot(weights.T, query_block, precision=lax.Precision.HIGHEST)
    key_grad = lax.psum_scatter(key_terms, "pb", scatter_dimension=0, tiled=True)
    query_grad = lax.psum_scatter(query_terms, "ka", scatter_dimension=0, tiled=True)
    totals = lax.psum(partial_value, ("pb", "ka"))
    grad_segments = backward_norm(query_unit, query_grad, query_inv)
    grad_futures = backward_norm(key_unit, key_grad, key_inv)
    return (grad_segments, grad_futures, totals / all_rows)


def solution(mesh):
    in_specs = (P(("pb", "ka"), None), P(("pb", "ka"), None), P("pb"), P(), P())
    out_specs = (P(("pb", "ka"), None), P(("pb", "ka"), None), P())
    return jax.shard_map(
        per_device, mesh=mesh, in_specs=in_specs, out_specs=out_specs, check_vma=False
    )
```

profile of v0, /device:TPU:24, one launch (start us, length us, event | category | flops | bytes accessed | tf_op | source)
XLA Modules:
  0.0 452.7 jit_solution(4869830445440605593)
XLA Ops:
  7.2 0.0 all-gather.3.cloned.1.call-start
  7.2 1.0 multiply_reduce_fusion.4
  8.2 1.5 broadcast_multiply_fusion.1
  9.7 0.0 all-gather.3.cloned.1.call-update
  9.8 0.0 all-gather.5.cloned.1.call-start
  9.8 1.0 multiply_reduce_fusion.3
  10.8 1.5 broadcast_multiply_fusion
  12.3 0.0 all-gather.5.cloned.1.call-update
  12.3 0.0 reduce-scatter.3.cloned.1.call-start
  13.7 0.7 compare_select_fusion.3
  14.4 61.5 %all-gather.3.cloned.1.call-done = f32[256,1024]{1,0:T(8,128)} async-done(((f32[16,1024]{1,0:T(8,128)}), f32[256,1024]{1,0:T(8,128)}) %all-gather.3.cloned.1.call-update) | async-done | bytes 1048592 | tf_op jit(solution)/shard_map/all_gather | solution.py:50
  75.9 135.5 %all-gather.5.cloned.1.call-done = f32[512,1024]{1,0:T(8,128)} async-done(((f32[16,1024]{1,0:T(8,128)}), f32[512,1024]{1,0:T(8,128)}) %all-gather.5.cloned.1.call-update) | async-done | bytes 2097168 | tf_op jit(solution)/shard_map/all_gather | solution.py:51
  211.4 0.0 copy-start
  211.4 5.2 %select_reduce_fusion = (f32[]{:T(128)}, f32[]{:T(128)}, f32[]{:T(128)}, f32[]{:T(128)}, f32[256,512]{1,0:T(8,128)S(1)}) fusion(s32[256]{0:T(256)S(1)} %compare_select_fusion.3, f32[]{:T(128)} %bitcast.9, f32[256,1024]{1,0:T(8,128)} %all-gather.3.cloned.1.call-done, f32[512,1024]{1,0:T(8,128)} %all-gather.5.cloned.1.call-done, f32[]{:T(128)} %bitcast), kind=kOutput, calls=%fused_computation.7 | convolution fusion | flops 1613365248 | bytes 3671064 | tf_op jit(solution)/shard_map/dot_general | solution.py:20
  216.7 0.0 copy-done
  216.7 3.0 convolution_multiply_fusion.1
  219.7 0.0 reduce-scatter.3.cloned.1.call-update
  219.7 0.0 copy-start.2
  219.7 0.0 reduce-scatter.5.cloned.1.call-start
  219.7 0.0 copy-done.1
  219.8 3.4 convolution_multiply_fusion
  223.1 0.0 reduce-scatter.5.cloned.1.call-update
  224.5 1.3 pad_maximum_fusion
  225.8 100.4 %psum.7 = f32[3]{0:T(128)S(1)} all-reduce(f32[3]{0:T(128)S(1)} %pad_maximum_fusion), channel_id=1, replica_groups=mesh['pb'=32,'ka'=16] {'pb','ka'}, use_global_device_ids=true, to_apply=%region_10.11 | all-reduce | flops 3 | bytes 24 | tf_op jit(solution)/shard_map/psum | solution.py:57
  326.1 0.5 broadcast_multiply_fusion.2
  326.7 0.0 copy-done.2
  326.7 1.0 multiply_reduce_fusion.2
  327.7 1.6 subtract_multiply_fusion.1
  329.2 114.3 %reduce-scatter.5.cloned.1.call-done = f32[16,1024]{1,0:T(8,128)} async-done(((f32[512,1024]{1,0:T(8,128)}), f32[16,1024]{1,0:T(8,128)}) %reduce-scatter.5.cloned.1.call-update) | async-done | bytes 65552 | tf_op jit(solution)/shard_map/reduce_scatter | solution.py:55
  443.6 0.0 copy-done.3
  443.6 1.0 multiply_reduce_fusion.1
  444.6 1.6 subtract_multiply_fusion
  (5 shorter events, 0.0 us)
Async XLA Ops:
  7.2 68.8 %all-gather.3.cloned.1.call-start = ((), (), s32[]{:S(2)}) async-start(), calls=%async_computation.2 | async-start | bytes 1114112 | tf_op jit(solution)/shard_map/all_gather | solution.py:50
  9.8 201.7 %all-gather.5.cloned.1.call-start = ((), (), s32[]{:S(2)}) async-start(), calls=%async_computation.3 | async-start | bytes 2162688 | tf_op jit(solution)/shard_map/all_gather | solution.py:51
  12.3 314.3 %reduce-scatter.3.cloned.1.call-start = ((), (), s32[]{:S(2)}) async-start(), calls=%async_computation.4 | async-start | bytes 1114112 | tf_op jit(solution)/shard_map/reduce_scatter | solution.py:56
  211.4 5.2 %copy-start = (f32[512,1024]{1,0:T(8,128)S(1)}, f32[512,1024]{1,0:T(8,128)}, u32[]{:S(2)}) copy-start(f32[512,1024]{1,0:T(8,128)} %all-gather.5.cloned.1.call-done) | copy-start | bytes 6291460
  216.7 3.1 copy-start.1
  219.7 107.0 %copy-start.2 = (f32[16,1024]{1,0:T(8,128)S(1)}, f32[16,1024]{1,0:T(8,128)}, u32[]{:S(2)}) copy-start(f32[16,1024]{1,0:T(8,128)} %param.5) | copy-start | bytes 196612
  219.7 223.9 %reduce-scatter.5.cloned.1.call-start = ((), (), s32[]{:S(2)}) async-start(), calls=%async_computation.5 | async-start | bytes 2162688 | tf_op jit(solution)/shard_map/reduce_scatter | solution.py:55
  223.1 220.5 %copy-start.3 = (f32[16,1024]{1,0:T(8,128)S(1)}, f32[16,1024]{1,0:T(8,128)}, u32[]{:S(2)}) copy-start(f32[16,1024]{1,0:T(8,128)} %param.6) | copy-start | bytes 196612
Sparse Core Ops, SparseCore 0:
  11.9 63.9 all-gather.2
  78.6 132.8 all-gather.4
  219.8 83.0 reduce-scatter.2
  305.7 137.7 reduce-scatter.4
where the time goes:
time: 454 us; the launch traced here: 453 us
  waiting for transfers between devices  311 us (69%)
  blocking collectives  100 us (22%)
  between operations  16.5 us (4%)
  other arithmetic  12.7 us (3%)
  matrix products  11.6 us (3%)
    all_gather x1, waiting for transfers between devices, per_device(): key_block = lax.all_gather(key_unit, 'pb', axis=0, tiled=True)  136 us
    reduce_scatter x1, waiting for transfers between devices, per_device(): lax.psum_scatter(key_terms, 'pb', scatter_dimension=0, tiled=True)  114 us
    psum x1, blocking collectives, per_device(): totals = lax.psum(partial_value, ('pb', 'ka'))  100 us
    all_gather x1, waiting for transfers between devices, per_device(): query_block = lax.all_gather(query_unit, 'ka', axis=0, tiled=True)  61.5 us
  transfers between devices with their start and end apart: 4, of which 3 were waited for; matrix products, arithmetic and copies ran while one was open for 2% of the time, Pallas kernels for 0%

commit v1 on v0

v1 whole, which is shorter than its diff:
```python
import jax
import jax.numpy as jnp
from jax import lax
from jax.experimental import pallas as pl
from jax.experimental.pallas import tpu as pltpu
from jax.sharding import PartitionSpec as P

MESH = pl.DeviceIdType.MESH
f32 = jnp.float32
bf16 = jnp.bfloat16
epsilon = 1e-06

NX, NY, NZ = 4, 4, 16
CHIPS = NX * NY
ROWS = 16
WIDTH = 1024
QUERIES = CHIPS * 2 * ROWS
KEYS = NZ * ROWS
FIRST = 12
HALVES = 2
HALF = ROWS // HALVES


def coordinates():
    pb = lax.axis_index("pb")
    ka = lax.axis_index("ka")
    return lax.rem(ka // 2, 2) * 2 + pb // NZ, ka // 4, lax.rem(pb, NZ), lax.rem(ka, 2)


def device(x, y, z, core):
    return (lax.rem(x, 2) * NZ + z, y * 4 + (x // 2) * 2 + core)


def chip_index(x, y):
    return lax.rem(x, 2) * 8 + y * 2 + x // 2


def chip_place(index):
    return (index % 2) * 2 + index // 8, (index // 2) % 4


def place_up(step):
    return 0 if step == 0 else 2 * step - 1


def place_down(step):
    return 2 * step


def split(value):
    high = value.astype(bf16)
    return high, (value - high.astype(f32)).astype(bf16)


def dot(a, b, dims):
    return lax.dot_general(a, b, (dims, ((), ())), preferred_element_type=f32)


def dot3(a_high, a_low, b_high, b_low, dims):
    return (dot(a_low, b_high, dims) + dot(a_high, b_low, dims)) + dot(a_high, b_high, dims)


NN = ((1,), (0,))
NT = ((1,), (1,))


def fold(value):
    rows = jnp.sum(value, axis=0, keepdims=True)
    return rows[:, 0:128] + rows[:, 128:256] + rows[:, 256:384] + rows[:, 384:512]


def unit_rows(value):
    inverse = lax.rsqrt(jnp.sum(value * value, axis=1, keepdims=True) + epsilon)
    return value * inverse, inverse


def kernel(
    segments, futures, pairs, log_scale, logit_bias,
    grad_segments, grad_futures, scalars,
    queries, queries_high, queries_low, keys, keys_high, keys_low,
    logits, weights, key_terms, query_terms,
    sums_up, sums_down, sibling_terms, plane_terms, targets,
    sums_mine, sums_pair, sums_plane, sums_line,
    gz_send, gz_recv, gp_send, gp_recv, gf_send, gf_recv, t_sem,
    rz_send, rz_recv, rs_send, rs_recv, rp_send, rp_recv,
    sp_sem, sl_send, sl_recv, sz_send, sz_recv,
):
    x, y, z, core = coordinates()
    me = chip_index(x, y)
    up = device(x, y, lax.rem(z + 1, NZ), core)
    down = device(x, y, lax.rem(z + NZ - 1, NZ), core)
    sibling = device(x, y, z, 1 - core)

    def remote(src, dst, send, recv, to):
        return pltpu.make_async_remote_copy(
            src_ref=src, dst_ref=dst, send_sem=send, recv_sem=recv, device_id=to, device_id_type=MESH
        )

    def plane_device(offset, other=False):
        return device(
            lax.rem(x + offset // 4, NX), lax.rem(y + offset % 4, NY), z, 1 - core if other else core
        )

    def plane_source(offset):
        return chip_index(lax.rem(x - offset // 4 + NX, NX), lax.rem(y - offset % 4 + NY, NY))

    sent = []

    def start(copy):
        copy.start()
        sent.append(copy)

    query_unit, query_inverse = unit_rows(segments[...])
    key_unit, key_inverse = unit_rows(futures[...])
    queries[me * 2 + core] = query_unit
    keys[0] = key_unit
    targets[lax.rem(x, 2)] = pairs[...]

    barrier = pltpu.get_barrier_semaphore()
    offsets = [1, 3, 4, 12, 5, 7, 13, 15, 2, 8, 6, 14, 9, 11, 10]
    greeted = [up, down, sibling] + [plane_device(d) for d in offsets]
    for other in greeted:
        pl.semaphore_signal(barrier, inc=1, device_id=other, device_id_type=MESH)
    pl.semaphore_wait(barrier, len(greeted))

    def gather_z(way, step, half):
        source = (place_up if way == 0 else place_down)(step - 1)
        target = (place_up if way == 0 else place_down)(step)
        rows = pl.ds(half * HALF, HALF)
        return remote(
            keys.at[source, rows], keys.at[target, rows],
            gz_send.at[way, step - 1, half], gz_recv.at[way, step - 1, half], up if way == 0 else down,
        )

    def gather_plane(offset):
        slot = queries.at[me * 2 + core]
        return remote(slot, slot, gp_send.at[offset], gp_recv.at[offset], plane_device(offset))

    def forward(offset):
        slot = queries.at[plane_source(offset) * 2 + core]
        return remote(slot, slot, gf_send.at[offset], gf_recv.at[offset], sibling)

    def step_z(step):
        for half in range(HALVES):
            for way in range(2):
                if way == 1 and step > 7:
                    continue
                if step > 1:
                    gather_z(way, step - 1, half).wait_recv()
                start(gather_z(way, step, half))

    step_z(1)
    start(forward(0))
    mine = targets.at[lax.rem(x, 2)]
    target_copy = remote(
        mine, mine, t_sem.at[0], t_sem.at[1], device(x + 1 - 2 * lax.rem(x, 2), y, z, core)
    )
    start(target_copy)
    for d in offsets:
        start(gather_plane(d))

    scale = jnp.exp(log_scale[...])
    bias = logit_bias[...]

    arrivals = list(offsets)

    def forward_next(count):
        for _ in range(min(count, len(arrivals))):
            d = arrivals.pop(0)
            gather_plane(d).wait_recv()
            start(forward(d))

    for step in range(2, 9):
        step_z(step)
        if step >= 4:
            forward_next(4)
    forward_next(15)
    target_copy.wait_recv()
    for d in [0] + offsets:
        forward(d).wait_recv()

    def split_keys(first, last):
        high, low = split(keys[first:last].reshape((last - first) * ROWS, WIDTH))
        keys_high[first * ROWS : last * ROWS] = high
        keys_low[first * ROWS : last * ROWS] = low

    def split_queries(first, last):
        high, low = split(queries[first:last].reshape((last - first) * ROWS, WIDTH))
        queries_high[first * ROWS : last * ROWS] = high
        queries_low[first * ROWS : last * ROWS] = low

    for i in range(0, 32, 8):
        split_queries(i, i + 8)
    split_keys(0, FIRST)

    def pair_block(first, last):
        a, b = first * ROWS, last * ROWS
        raw = dot3(
            keys_high[a:b], keys_low[a:b], queries_high[...], queries_low[...], NT
        )
        value = scale * raw + bias
        row = lax.broadcasted_iota(jnp.int32, (b - a, 1), 0) + a
        place = row // ROWS
        step = (place + 1) // 2
        line = lax.rem(z + jnp.where(place % 2 == 1, NZ - step, step), NZ)
        ka = lax.axis_index("ka")
        key_row = (lax.rem(x, 2) * NZ + line) * (ROWS * 16) + ka * ROWS + row % ROWS
        target = jnp.concatenate([targets[0], targets[1]], axis=1)
        hit = key_row == target
        small = jnp.exp(-jnp.abs(value))
        sigmoid = jnp.where(value >= 0, f32(1.0), small) / (f32(1.0) + small)
        weight = sigmoid - hit.astype(f32)
        softplus = jnp.maximum(value, f32(0.0)) + jnp.log1p(small)
        weights[a:b] = scale * weight
        loss = fold(softplus - jnp.where(hit, value, f32(0.0)))
        by_scale = fold(weight * (value - bias))
        by_bias = fold(weight)
        return jnp.concatenate([loss, by_scale, by_bias, jnp.zeros((5, 128), f32)], axis=0)

    def key_block(first, last):
        a, b = first * ROWS, last * ROWS
        high, low = split(weights[a:b])
        out = dot3(high, low, queries_high[...], queries_low[...], NN)
        key_terms[first:last] = out.reshape(last - first, ROWS, WIDTH)

    totals = pair_block(0, FIRST)
    for half in range(HALVES):
        gather_z(0, 8, half).wait_recv()
        gather_z(1, 7, half).wait_recv()
    split_keys(FIRST, NZ)
    totals = totals + pair_block(FIRST, NZ)
    key_block(FIRST, NZ)

    def sum_z(way, step, half):
        rows = pl.ds(half * HALF, HALF)
        if way == 0:
            place = place_down(8 - step) if step > 0 else place_up(8)
            land = sums_up
        else:
            place = place_up(7 - step)
            land = sums_down
        return place, land, remote(
            key_terms.at[place, rows], land.at[step, rows],
            rz_send.at[way, step, half], rz_recv.at[way, step, half], up if way == 0 else down,
        )

    def reduce_z(step):
        for half in range(HALVES):
            rows = slice(half * HALF, half * HALF + HALF)
            for way in range(2):
                if way == 1 and step > 6:
                    continue
                place, land, copy = sum_z(way, step, half)
                if step > 0:
                    sum_z(way, step - 1, half)[2].wait_recv()
                    key_terms[place, rows] = key_terms[place, rows] + land[step - 1, rows]
                start(copy)

    reduce_z(0)

    sums_mine[...] = totals
    pair_sums = remote(sums_mine, sums_pair, sp_sem.at[0], sp_sem.at[1], sibling)
    start(pair_sums)

    key_block(0, FIRST)
    reduce_z(1)

    def query_block(first, last):
        a, b = first * 2 * ROWS, last * 2 * ROWS
        high, low = split(weights[:, a:b].T)
        out = dot3(high, low, keys_high[...], keys_low[...], NN)
        query_terms[first:last] = out.reshape(last - first, 2, ROWS, WIDTH)

    def sum_sibling(index):
        return remote(
            query_terms.at[index, 1 - core], sibling_terms.at[index], rs_send.at[index], rs_recv.at[index], sibling
        )

    def sum_plane(index):
        cx, cy = chip_place(index)
        return remote(
            query_terms.at[index, core], plane_terms.at[me], rp_send.at[index], rp_recv.at[me],
            device(jnp.int32(cx), jnp.int32(cy), z, core),
        )

    def plane_arrival(index):
        return remote(
            query_terms.at[index, core], plane_terms.at[index], rp_send.at[index], rp_recv.at[index], sibling
        )

    def send_plane(first, last):
        for index in range(first, last):
            sum_sibling(index).wait_recv()
            query_terms[index, core] = query_terms[index, core] + sibling_terms[index]

            @pl.when(index != me)
            def _():
                sum_plane(index).start()

    GROUP = 4
    for first in range(0, CHIPS, GROUP):
        query_block(first, first + GROUP)
        for index in range(first, first + GROUP):
            start(sum_sibling(index))
        if first >= GROUP:
            send_plane(first - GROUP, first)
        if first % (2 * GROUP) == GROUP:
            reduce_z(2 + first // (2 * GROUP))
        if first == 0:
            pair_sums.wait_recv()
            sums_plane[me] = sums_mine[...] + sums_pair[...]
            for d in offsets:
                start(remote(sums_plane.at[me], sums_plane.at[me], sl_send.at[d], sl_recv.at[d], plane_device(d)))
    send_plane(CHIPS - GROUP, CHIPS)
    reduce_z(4)
    for d in offsets:
        slot = sums_plane.at[plane_source(d)]
        remote(slot, slot, sl_send.at[d], sl_recv.at[d], sibling).wait_recv()
    sums_line[z] = jnp.sum(sums_plane[...], axis=0)
    for d in range(1, NZ):
        slot = sums_line.at[z]
        start(remote(slot, slot, sz_send.at[d], sz_recv.at[d], device(x, y, lax.rem(z + d, NZ), core)))
    reduce_z(5)
    reduce_z(6)
    reduce_z(7)

    def backward(direction, grad, inverse):
        return (grad - direction * jnp.sum(direction * grad, axis=1, keepdims=True)) * inverse

    plane_terms[me] = query_terms[me, core]
    for index in range(CHIPS):

        @pl.when(index != me)
        def _():
            plane_arrival(index).wait_recv()

    query_grad = jnp.sum(plane_terms[...], axis=0)
    grad_segments[...] = backward(query_unit, query_grad, query_inverse)

    for d in range(1, NZ):
        slot = sums_line.at[lax.rem(z - d + NZ, NZ)]
        remote(slot, slot, sz_send.at[d], sz_recv.at[d], sibling).wait_recv()
    total = jnp.sum(sums_line[...], axis=0) * f32(1.0 / 8192)
    for i in range(3):
        scalars[i] = jnp.sum(total[i : i + 1, :])

    for half in range(HALVES):
        sum_z(0, 7, half)[2].wait_recv()
        sum_z(1, 6, half)[2].wait_recv()
    key_grad = key_terms[0] + sums_up[7] + sums_down[6]
    grad_futures[...] = backward(key_unit, key_grad, key_inverse)

    for copy in sent:
        copy.wait_send()
    for index in range(CHIPS):

        @pl.when(index != me)
        def _():
            sum_plane(index).wait_send()


def per_device(segments, futures, pair_index, log_scale, logit_bias):
    dma = pltpu.SemaphoreType.DMA
    vmem = pltpu.VMEM
    block = (ROWS, WIDTH)
    in_vmem = pl.BlockSpec(memory_space=pltpu.VMEM)
    return pl.pallas_call(
        kernel,
        out_shape=(
            jax.ShapeDtypeStruct(block, f32),
            jax.ShapeDtypeStruct(block, f32),
            jax.ShapeDtypeStruct((3,), f32),
        ),
        in_specs=[in_vmem] * 5,
        out_specs=(in_vmem, in_vmem, pl.BlockSpec(memory_space=pltpu.SMEM)),
        scratch_shapes=[
            vmem((CHIPS * 2,) + block, f32),
            vmem((QUERIES, WIDTH), bf16),
            vmem((QUERIES, WIDTH), bf16),
            vmem((NZ,) + block, f32),
            vmem((KEYS, WIDTH), bf16),
            vmem((KEYS, WIDTH), bf16),
            vmem((KEYS, QUERIES), f32),
            vmem((KEYS, QUERIES), f32),
            vmem((NZ,) + block, f32),
            vmem((CHIPS, 2) + block, f32),
            vmem((8,) + block, f32),
            vmem((8,) + block, f32),
            vmem((CHIPS,) + block, f32),
            vmem((CHIPS,) + block, f32),
            vmem((2, 1, 256), jnp.int32),
            vmem((8, 128), f32),
            vmem((8, 128), f32),
            vmem((CHIPS, 8, 128), f32),
            vmem((NZ, 8, 128), f32),
            dma((2, 8, HALVES)), dma((2, 8, HALVES)),
            dma((CHIPS,)), dma((CHIPS,)),
            dma((CHIPS,)), dma((CHIPS,)),
            dma((2,)),
            dma((2, 8, HALVES)), dma((2, 8, HALVES)),
            dma((CHIPS,)), dma((CHIPS,)),
            dma((CHIPS,)), dma((CHIPS,)),
            dma((2,)),
            dma((CHIPS,)), dma((CHIPS,)),
            dma((NZ,)), dma((NZ,)),
        ],
        compiler_params=pltpu.CompilerParams(
            collective_id=0, has_side_effects=True, vmem_limit_bytes=40 << 20
        ),
    )(
        segments,
        futures,
        pair_index.reshape(1, 256),
        log_scale.reshape(1, 1),
        logit_bias.reshape(1, 1),
    )


def solution(mesh):
    in_specs = (P(("pb", "ka"), None), P(("pb", "ka"), None), P("pb"), P(), P())
    out_specs = (P(("pb", "ka"), None), P(("pb", "ka"), None), P())
    return jax.shard_map(
        per_device, mesh=mesh, in_specs=in_specs, out_specs=out_specs, check_vma=False
    )
```

time: 454 us -> 78.6 us (0.17)
  waiting for transfers between devices: 311 us -> 0 us
  blocking collectives: 100 us -> 0 us
  Pallas kernels: 0 us -> 71.4 us
  between operations: 16.5 us -> 1.94 us
  other arithmetic: 12.7 us -> 0 us
  matrix products: 11.6 us -> 0 us
    all_gather x2 -> x0, waiting for transfers between devices: 197 us -> none  [the longest x1 136 us: per_device(): key_block = lax.all_gather(key_unit, 'pb', axis=0, tiled=True)]
    reduce_scatter x2 -> x0, waiting for transfers between devices: 114 us -> none  [the longest x1 114 us: per_device(): lax.psum_scatter(key_terms, 'pb', scatter_dimension=0, tiled=True)]
    psum x1 -> x0, blocking collectives: 100 us -> none  [per_device(): totals = lax.psum(partial_value, ('pb', 'ka'))]
    pallas_call x0 -> x1, Pallas kernels: none -> 71.4 us  [per_device(): pl.pallas_call(kernel, out_shape=(jax.ShapeDtypeStruct(block, f32), jax.S...]
    dot_general x3 -> x0, matrix products: 11.6 us -> none  [the longest x1 5.22 us: tile_terms(): jnp.dot(query_block, key_piece.T, precision=lax.Precision.HIGHEST)]
    mul x4 -> x0, other arithmetic: 6.2 us -> none  [the longest x2 3.1 us: backward_norm(): (grad_dir - direction * jnp.sum(direction * grad_dir, axis=1, keepdims=Tr...]
  transfers between devices with their start and end apart: 4 -> 0, of which waited for: 3 -> 0; matrix products, arithmetic and copies ran while one was open for 2% -> 0% of each run, Pallas kernels for 0% -> 0%
where the time goes in v1:
time: 78.6 us; the launch traced here: 77.5 us
  Pallas kernels  71.4 us (91%)
  local copies, waits for them, and re-layouts  4.12 us (5%)
  between operations  1.94 us (2%)
    pallas_call x1, Pallas kernels, per_device(): pl.pallas_call(kernel, out_shape=(jax.ShapeDtypeStruct(block, f32), jax.S...  71.4 us
    unnamed x9, local copies, waits for them, and re-layouts  4.12 us

profile of v1, /device:TPU:24, one launch (start us, length us, event | category | flops | bytes accessed | tf_op | source)
XLA Modules:
  0.0 77.5 jit_solution(12634572535352003116)
XLA Ops:
  1.9 0.0 copy-start.2
  1.9 0.7 copy-done.2
  2.6 0.0 copy-start
  2.6 0.8 %copy-done = f32[16,1024]{1,0:T(8,128)S(1)} copy-done((f32[16,1024]{1,0:T(8,128)S(1)}, f32[16,1024]{1,0:T(8,128)}, u32[]{:S(2)}) %copy-start) | copy-done | bytes 65560
  3.4 0.0 copy-start.1
  3.4 0.8 %copy-done.1 = f32[16,1024]{1,0:T(8,128)S(1)} copy-done((f32[16,1024]{1,0:T(8,128)S(1)}, f32[16,1024]{1,0:T(8,128)}, u32[]{:S(2)}) %copy-start.1) | copy-done | bytes 65560
  4.3 71.4 %shard_map.76 = (f32[16,1024]{1,0:T(8,128)S(1)}, f32[16,1024]{1,0:T(8,128)S(1)}, f32[3]{0:T(128)S(1)}) custom-call(f32[16,1024]{1,0:T(8,128)S(1)} %copy-done, f32[16,1024]{1,0:T(8,128)S(1)} %copy-done.1, s32[1,256]{1,0:T(1,128)S(1)} %bitcast.5, f32[1,1]{1,0:T(1,128)} %bitcast.3.log_scale, f32[1,1]{1,0:T(1,128)} %bitcast.4.logit_bias), custom_call_target="tpu_custom_call" | custom-call | tf_op jit(solution)/shard_map/pallas_call | solution.py:367
  75.7 0.6 copy.13
  76.4 0.6 copy.14
  77.0 0.5 copy.15
Async XLA Ops:
  1.9 0.7 copy-start.2
  2.6 0.8 %copy-start = (f32[16,1024]{1,0:T(8,128)S(1)}, f32[16,1024]{1,0:T(8,128)}, u32[]{:S(2)}) copy-start(f32[16,1024]{1,0:T(8,128)} %segments.1) | copy-start | bytes 196612
  3.4 0.8 %copy-start.1 = (f32[16,1024]{1,0:T(8,128)S(1)}, f32[16,1024]{1,0:T(8,128)}, u32[]{:S(2)}) copy-start(f32[16,1024]{1,0:T(8,128)} %futures.1) | copy-start | bytes 196612

commit v2 on v0

v2 whole, which is shorter than its diff:
```python
import jax
import jax.numpy as jnp
from jax import lax
from jax.experimental import pallas as pl
from jax.experimental.pallas import tpu as pltpu
from jax.sharding import PartitionSpec as P

MESH = pl.DeviceIdType.MESH
f32 = jnp.float32
bf16 = jnp.bfloat16
epsilon = 1e-06

NX, NY, NZ = 4, 4, 16
RING = NZ // 2
ROWS = 16
WIDTH = 1024
CHIPS = 16
QUERIES = CHIPS * 2 * ROWS
KEYS = CHIPS * ROWS
FIRST = 10
HALVES = 2
HALF = ROWS // HALVES
FAR = 4
KZ, KX, QP, QY, QS, TG, RX, RZ, RS, RY, RP, SL, SW, SR, SY = range(15)


def coordinates():
    pb = lax.axis_index("pb")
    ka = lax.axis_index("ka")
    return lax.rem(ka // 2, 2) * 2 + pb // NZ, ka // 4, lax.rem(pb, NZ), lax.rem(ka, 2)


def device(x, y, z, core):
    return (lax.rem(x, 2) * NZ + z, y * 4 + (x // 2) * 2 + core)


def place_of(way, step):
    return 0 if step == 0 else 7 if step == FAR else 2 * step - 1 + way


def has(way, step, half):
    return step < FAR or way == half


def split(value):
    high = value.astype(bf16)
    return high, (value - high.astype(f32)).astype(bf16)


def dot(a, b, dims):
    return lax.dot_general(a, b, (dims, ((), ())), preferred_element_type=f32)


def dot3(a_high, a_low, b_high, b_low, dims):
    return (dot(a_low, b_high, dims) + dot(a_high, b_low, dims)) + dot(a_high, b_high, dims)


NN = ((1,), (0,))
NT = ((1,), (1,))


def fold(value):
    rows = jnp.sum(value, axis=0, keepdims=True)
    return rows[:, 0:128] + rows[:, 128:256] + rows[:, 256:384] + rows[:, 384:512]


def unit_rows(value):
    inverse = lax.rsqrt(jnp.sum(value * value, axis=1, keepdims=True) + epsilon)
    return value * inverse, inverse


def backward(direction, grad, inverse):
    return (grad - direction * jnp.sum(direction * grad, axis=1, keepdims=True)) * inverse


def kernel(
    segments_hbm, futures_hbm, pairs_hbm, log_scale, logit_bias,
    grad_segments, grad_futures, scalars,
    segments, futures, pairs,
    queries, queries_high, queries_low, keys, keys_high, keys_low,
    weights, weights_high, weights_low, key_terms, x_terms, ring_terms,
    query_terms, sibling_terms, y_terms, pair_terms, z_terms, targets,
    sums_line, sums_two, sums_row, sums_y,
    in_sem, send, kz_recv, kx_recv, qp_recv, qy_recv, qs_recv,
    rx_recv, rz_recv, rs_recv, ry_recv, rp_recv, once_recv,
):
    x, y, z, core = coordinates()
    odd_x, odd_z = lax.rem(x, 2), lax.rem(z, 2)
    key_x = x + 1 - 2 * odd_x
    query_x = lax.rem(x + 2 * odd_x + NX - 1, NX)
    pair_z = z + 1 - 2 * odd_z

    sibling = device(x, y, z, 1 - core)
    key_partner = device(key_x, y, z, core)
    query_partner = device(query_x, y, z, core)
    z_partner = device(x, y, pair_z, core)

    def y_device(offset):
        return device(x, lax.rem(y + offset, NY), z, core)

    def ring_device(steps, column=None):
        return device(x if column is None else column, y, lax.rem(z + 2 * steps + NZ, NZ), core)

    def row_device(offset, other):
        return device(lax.rem(x + offset, NX), y, z, 1 - core if other else core)

    def remote(src, dst, kind, recv, to):
        return pltpu.make_async_remote_copy(
            src_ref=src, dst_ref=dst, send_sem=send.at[kind], recv_sem=recv, device_id=to, device_id_type=MESH
        )

    def await_recv(ref, kind, recv):
        remote(ref, ref, kind, recv, sibling).wait_recv()

    def await_send(ref, kind):
        remote(ref, ref, kind, once_recv.at[0], sibling).wait_send()

    barrier = pltpu.get_barrier_semaphore()
    target_peers = [z_partner, query_partner, device(query_x, y, pair_z, core)]
    row_peers = [(d, other) for d in range(NX) for other in (False, True) if d or other]
    greeted = [ring_device(way, column) for way in (1, -1) for column in (None, key_x)] + [z_partner, target_peers[2]]
    greeted += [y_device(d) for d in range(1, NY)] + [row_device(*p) for p in row_peers]
    for other in greeted:
        pl.semaphore_signal(barrier, inc=1, device_id=other, device_id_type=MESH)

    loads = [
        pltpu.make_async_copy(futures_hbm, futures, in_sem.at[0]),
        pltpu.make_async_copy(segments_hbm, segments, in_sem.at[1]),
        pltpu.make_async_copy(pairs_hbm, pairs, in_sem.at[2]),
    ]
    for load in loads:
        load.start()

    def column(combo):
        w = 1 - odd_z if combo in (1, 3) else odd_z
        v = 1 - odd_x if combo in (2, 3) else odd_x
        return w * 2 + v

    def query_slot(combo, offset, c):
        return column(combo) * 8 + lax.rem(y - offset + NY, NY) * 2 + c

    loads[0].wait()
    key_unit, key_inverse = unit_rows(futures[...])
    keys[0] = key_unit
    loads[1].wait()
    query_unit, query_inverse = unit_rows(segments[...])
    queries[query_slot(0, 0, core)] = query_unit
    loads[2].wait()
    mine = pairs[...]
    parts = [
        jnp.where(x // 2 == 0, mine[:, 64 * i : 64 * i + 32], mine[:, 64 * i + 32 : 64 * i + 64]) for i in range(NY)
    ]
    targets[column(0)] = jnp.concatenate(parts, axis=1)
    pl.semaphore_wait(barrier, len(greeted))

    def half_rows(half):
        return pl.ds(half * HALF, HALF)

    def gather_ring(way, step, half):
        rows = half_rows(half)
        return remote(
            keys.at[2 * place_of(way, step - 1), rows], keys.at[2 * place_of(way, step), rows],
            KZ, kz_recv.at[way, step - 1, half], ring_device(1 if way == 0 else -1),
        )

    def gather_far(way):
        rows = half_rows(way)
        return remote(
            keys.at[2 * place_of(way, FAR - 1), rows], keys.at[2 * RING - 1, rows],
            KZ, kx_recv.at[RING - 1], ring_device(1 if way == 0 else -1, key_x),
        )

    def gather_x(place):
        return remote(keys.at[2 * place], keys.at[2 * place + 1], KX, kx_recv.at[place], key_partner)

    def step_ring(step):
        for half in range(HALVES):
            for way in range(2):
                if step > 0 and has(way, step, half):
                    gather_ring(way, step, half).wait_recv()
                if step < FAR and has(way, step + 1, half):
                    gather_ring(way, step + 1, half).start()
                    if step + 1 == FAR:
                        gather_far(way).start()
        if step < FAR:
            for way in range(2):
                if step > 0 or way == 0:
                    gather_x(place_of(way, step)).start()

    def await_x(place):
        await_recv(keys.at[2 * place + 1], KX, kx_recv.at[place])

    def gather_partner(combo):
        slot = queries.at[query_slot(0 if combo < 3 else 1, 0, core)]
        return remote(slot, slot, QP, qp_recv.at[combo], z_partner if combo == 1 else query_partner)

    def gather_y(combo, offset):
        slot = queries.at[query_slot(combo, 0, core)]
        return remote(slot, slot, QY, qy_recv.at[combo], y_device(offset))

    def gather_sibling(combo, offset):
        slot = queries.at[query_slot(combo, offset, core)]
        return remote(slot, slot, QS, qs_recv.at[combo], sibling)

    def split_query(slot):
        high, low = split(queries[slot])
        rows = pl.ds(pl.multiple_of(slot * ROWS, ROWS), ROWS)
        queries_high[rows] = high
        queries_low[rows] = low

    def split_keys(first, last):
        high, low = split(keys[first:last].reshape((last - first) * ROWS, WIDTH))
        keys_high[first * ROWS : last * ROWS] = high
        keys_low[first * ROWS : last * ROWS] = low

    def spread(combo):
        if combo > 0:
            gather_partner(combo).wait_recv()
        if combo == 1:
            gather_partner(3).start()
        for offset in (2, 1, 3):
            gather_y(combo, offset).start()
        gather_sibling(combo, 0).start()
        split_query(query_slot(combo, 0, core))

    def take_y(combo):
        await_recv(queries.at[pl.ds(0, 3)], QY, qy_recv.at[combo])
        for offset in (1, 3, 2):
            gather_sibling(combo, offset).start()
        for offset in (1, 3, 2):
            split_query(query_slot(combo, offset, core))

    def take_sibling(combo):
        await_recv(queries.at[pl.ds(0, 4)], QS, qs_recv.at[combo])
        for offset in (0, 1, 3, 2):
            split_query(query_slot(combo, offset, 1 - core))

    step_ring(0)
    gather_partner(1).start()
    gather_partner(2).start()
    spread(0)
    mine_target = targets.at[column(0)]
    for to in target_peers:
        remote(mine_target, mine_target, TG, once_recv.at[0], to).start()
    scale = jnp.exp(log_scale[...])
    bias = logit_bias[...]
    spread(1)
    spread(2)
    step_ring(1)
    take_y(0)
    spread(3)
    step_ring(2)
    take_y(1)
    take_sibling(0)
    take_y(2)
    step_ring(3)
    take_sibling(1)
    take_y(3)
    take_sibling(2)
    take_sibling(3)
    await_recv(targets.at[pl.ds(0, 3)], TG, once_recv.at[0])

    def pair_block(first, last):
        a, b = first * ROWS, last * ROWS
        raw = dot3(
            keys_high[a:b], keys_low[a:b], queries_high[...], queries_low[...], NT
        )
        value = scale * raw + bias
        row = lax.broadcasted_iota(jnp.int32, (b - a, 1), 0) + a
        place = row // (2 * ROWS)
        step = (place + 1) // 2
        line = lax.rem(z + 2 * jnp.where(place % 2 == 1, RING - step, step), NZ)
        low_x = jnp.where(row // ROWS % 2 == 1, 1 - odd_x, odd_x)
        key_row = (low_x * NZ + line) * (ROWS * 16) + lax.axis_index("ka") * ROWS + row % ROWS
        target = jnp.concatenate([targets[i] for i in range(4)], axis=1)
        hit = key_row == target
        small = jnp.exp(-jnp.abs(value))
        sigmoid = jnp.where(value >= 0, f32(1.0), small) / (f32(1.0) + small)
        weight = sigmoid - hit.astype(f32)
        softplus = jnp.maximum(value, f32(0.0)) + jnp.log1p(small)
        weights[a:b] = scale * weight
        loss = fold(softplus - jnp.where(hit, value, f32(0.0)))
        by_scale = fold(weight * (value - bias))
        by_bias = fold(weight)
        return jnp.concatenate([loss, by_scale, by_bias, jnp.zeros((5, 128), f32)], axis=0)

    def key_block(first, last):
        a, b = first * ROWS, last * ROWS
        high, low = split(weights[a:b])
        out = dot3(high, low, queries_high[...], queries_low[...], NN)
        key_terms[first:last] = out.reshape(last - first, ROWS, WIDTH)

    for place in range(FIRST // 2):
        await_x(place)
    split_keys(0, FIRST)
    totals = pair_block(0, FIRST)
    step_ring(4)
    for place in range(FIRST // 2, RING):
        await_x(place)
    split_keys(FIRST, CHIPS)
    totals = totals + pair_block(FIRST, CHIPS)
    key_block(FIRST, CHIPS)

    def sum_x(place):
        return remote(key_terms.at[2 * place + 1], x_terms.at[place], RX, rx_recv.at[place], key_partner)

    def sum_far(way):
        rows = half_rows(way)
        return remote(
            key_terms.at[2 * RING - 1, rows], x_terms.at[RING - 1, rows],
            RX, rx_recv.at[RING - 1 + way], ring_device(-1 if way == 0 else 1, key_x),
        )

    def sum_ring(way, step, half):
        rows = half_rows(half)
        return remote(
            key_terms.at[2 * place_of(way, step), rows], ring_terms.at[way, step - 1, rows],
            RZ, rz_recv.at[way, step - 1, half], ring_device(-1 if way == 0 else 1),
        )

    def start_x(*places):
        for place in places:
            sum_x(place).start()

    def start_far():
        for way in range(2):
            sum_ring(way, FAR, way).start()
            sum_far(way).start()

    def reduce_ring(step):
        for half in range(HALVES):
            rows = half_rows(half)
            for way in range(2):
                place = place_of(way, step)
                if half == 0:
                    sum_x(place).wait_recv()
                total = key_terms[2 * place, rows] + x_terms[place, rows]
                if has(way, step + 1, half):
                    sum_ring(way, step + 1, half).wait_recv()
                    total = total + ring_terms[way, step, rows]
                if step + 1 == FAR and way == half:
                    sum_far(way).wait_recv()
                    total = total + x_terms[RING - 1, rows]
                key_terms[2 * place, rows] = total
                sum_ring(way, step, half).start()

    start_far()
    start_x(5, 6)

    def start_line():
        slot = sums_line.at[z // 2]
        sums_line[z // 2] = totals
        for d in range(1, RING):
            remote(slot, slot, SL, once_recv.at[1], ring_device(d)).start()

    def start_two():
        await_recv(sums_line.at[pl.ds(0, RING - 1)], SL, once_recv.at[1])
        sums_two[odd_z] = jnp.sum(sums_line[...], axis=0)
        slot = sums_two.at[odd_z]
        remote(slot, slot, SW, once_recv.at[2], z_partner).start()

    def start_row():
        await_recv(sums_two.at[0], SW, once_recv.at[2])
        sums_row[x * 2 + core] = sums_two[0] + sums_two[1]
        slot = sums_row.at[x * 2 + core]
        for p in row_peers:
            remote(slot, slot, SR, once_recv.at[3], row_device(*p)).start()

    def start_column():
        await_recv(sums_row.at[pl.ds(0, 2 * NX - 1)], SR, once_recv.at[3])
        sums_y[y] = jnp.sum(sums_row[...], axis=0)
        slot = sums_y.at[y]
        for d in range(1, NY):
            remote(slot, slot, SY, once_recv.at[4], y_device(d)).start()

    def finish_scalars():
        await_recv(sums_y.at[pl.ds(0, NY - 1)], SY, once_recv.at[4])
        total = jnp.sum(sums_y[...], axis=0) * f32(1.0 / 8192)
        scalars[...] = jnp.broadcast_to(jnp.sum(total, axis=1, keepdims=True), scalars.shape)

    def query_block(combo):
        rows = pl.ds(pl.multiple_of(column(combo) * 8 * ROWS, 8 * ROWS), 8 * ROWS)
        out = dot3(weights_high[rows], weights_low[rows], keys_high[...], keys_low[...], NN)
        query_terms[combo] = out.reshape(NY, 2, ROWS, WIDTH)
        for place in range(NY):
            remote(
                query_terms.at[combo, place, 1 - core], sibling_terms.at[combo, place],
                RS, rs_recv.at[combo], sibling,
            ).start()

    def sum_y(combo, offset):
        return remote(
            query_terms.at[combo, lax.rem(y + offset, NY), core], y_terms.at[combo, offset],
            RY, ry_recv.at[combo], y_device(offset),
        )

    def start_y(combo):
        await_recv(sibling_terms.at[combo], RS, rs_recv.at[combo])
        for offset in (2, 1, 3, 0):
            place = lax.rem(y + offset, NY)
            query_terms[combo, place, core] = query_terms[combo, place, core] + sibling_terms[combo, place]
            if offset > 0:
                sum_y(combo, offset).start()

    def take_column(combo):
        await_recv(y_terms.at[combo, pl.ds(1, 3)], RY, ry_recv.at[combo])
        return ((y_terms[combo, 1] + y_terms[combo, 3]) + y_terms[combo, 2]) + query_terms[combo, y, core]

    def sum_partner(combo):
        return remote(
            pair_terms.at[combo], z_terms.at[combo], RP, rp_recv.at[combo],
            z_partner if combo == 1 else query_partner,
        )

    start_line()
    high, low = split(weights[...].T)
    weights_high[...] = high
    weights_low[...] = low
    query_block(3)
    query_block(2)
    start_y(3)
    query_block(1)
    start_y(2)
    query_block(0)
    start_y(1)
    reduce_ring(3)
    key_block(0, FIRST)
    start_x(3, 4, 1, 2, 0)
    start_y(0)
    start_two()
    reduce_ring(2)
    for combo in (3, 2):
        pair_terms[combo] = take_column(combo)
        sum_partner(combo).start()
    start_row()
    near = take_column(1)
    sum_partner(3).wait_recv()
    pair_terms[1] = near + z_terms[3]
    sum_partner(1).start()
    reduce_ring(1)
    start_column()

    query_grad = take_column(0)
    sum_partner(2).wait_recv()
    query_grad = query_grad + z_terms[2]
    sum_partner(1).wait_recv()
    query_grad = query_grad + z_terms[1]
    grad_segments[...] = backward(query_unit, query_grad, query_inverse)

    finish_scalars()

    sum_x(0).wait_recv()
    for half in range(HALVES):
        for way in range(2):
            sum_ring(way, 1, half).wait_recv()
    key_grad = (key_terms[0] + x_terms[0]) + (ring_terms[0, 0] + ring_terms[1, 0])
    grad_futures[...] = backward(key_unit, key_grad, key_inverse)

    def blocks(ref, count):
        return ref.at[pl.ds(0, count)]

    await_send(blocks(keys, 8), KZ)
    await_send(blocks(keys, 7), KX)
    await_send(blocks(queries, 3), QP)
    await_send(blocks(queries, 12), QY)
    await_send(blocks(queries, 16), QS)
    await_send(blocks(targets, 3), TG)
    await_send(blocks(key_terms, 8), RX)
    await_send(blocks(key_terms, 7), RZ)
    await_send(blocks(queries, 16), RS)
    await_send(blocks(queries, 12), RY)
    await_send(blocks(queries, 3), RP)
    await_send(blocks(sums_line, RING - 1), SL)
    await_send(sums_two.at[0], SW)
    await_send(blocks(sums_row, 2 * NX - 1), SR)
    await_send(blocks(sums_y, NY - 1), SY)


def per_device(segments, futures, pair_index, log_scale, logit_bias):
    dma = pltpu.SemaphoreType.DMA
    vmem = pltpu.VMEM
    block = (ROWS, WIDTH)
    sums = (8, 128)
    in_vmem = pl.BlockSpec(memory_space=pltpu.VMEM)
    in_hbm = pl.BlockSpec(memory_space=pltpu.HBM)

    grad_segments, grad_futures, scalars = pl.pallas_call(
        kernel,
        out_shape=(
            jax.ShapeDtypeStruct(block, f32),
            jax.ShapeDtypeStruct(block, f32),
            jax.ShapeDtypeStruct(sums, f32),
        ),
        in_specs=[in_hbm] * 3 + [in_vmem] * 2,
        out_specs=(in_vmem, in_vmem, in_vmem),
        scratch_shapes=[
            vmem(block, f32),
            vmem(block, f32),
            vmem((1, 256), jnp.int32),
            vmem((CHIPS * 2,) + block, f32),
            vmem((QUERIES, WIDTH), bf16),
            vmem((QUERIES, WIDTH), bf16),
            vmem((CHIPS,) + block, f32),
            vmem((KEYS, WIDTH), bf16),
            vmem((KEYS, WIDTH), bf16),
            vmem((KEYS, QUERIES), f32),
            vmem((QUERIES, KEYS), bf16),
            vmem((QUERIES, KEYS), bf16),
            vmem((CHIPS,) + block, f32),
            vmem((RING,) + block, f32),
            vmem((2, FAR) + block, f32),
            vmem((4, NY, 2) + block, f32),
            vmem((4, NY) + block, f32),
            vmem((4, NY) + block, f32),
            vmem((4,) + block, f32),
            vmem((4,) + block, f32),
            vmem((4, 1, 128), jnp.int32),
            vmem((RING,) + sums, f32),
            vmem((2,) + sums, f32),
            vmem((2 * NX,) + sums, f32),
            vmem((NY,) + sums, f32),
            dma((3,)),
            dma((15,)),
            dma((2, FAR, HALVES)),
            dma((RING,)),
            dma((4,)),
            dma((4,)),
            dma((4,)),
            dma((RING + 1,)),
            dma((2, FAR, HALVES)),
            dma((4,)),
            dma((4,)),
            dma((4,)),
            dma((5,)),
        ],
        compiler_params=pltpu.CompilerParams(
            collective_id=0, has_side_effects=True, vmem_limit_bytes=40 << 20
        ),
    )(
        segments,
        futures,
        pair_index.reshape(1, 256),
        log_scale.reshape(1, 1),
        logit_bias.reshape(1, 1),
    )
    return grad_segments, grad_futures, scalars[:3, 0]


def solution(mesh):
    in_specs = (P(("pb", "ka"), None), P(("pb", "ka"), None), P("pb"), P(), P())
    out_specs = (P(("pb", "ka"), None), P(("pb", "ka"), None), P())
    return jax.shard_map(
        per_device, mesh=mesh, in_specs=in_specs, out_specs=out_specs, check_vma=False
    )
```

time: 454 us -> 64.1 us (0.14)
  the two profiles are of different devices: /device:TPU:24 before, /device:TPU:3 now
where the time goes in v2:
time: 64.1 us; the launch traced here: 63.9 us
  Pallas kernels  57.7 us (90%)
  local copies, waits for them, and re-layouts  4.23 us (7%)
  between operations  1.94 us (3%)
    pallas_call x1, Pallas kernels, per_device(): pl.pallas_call(kernel, out_shape=(jax.ShapeDtypeStruct(block, f32), jax.S...  57.7 us
    unnamed x8, local copies, waits for them, and re-layouts  3.61 us

profile of v2, /device:TPU:3, one launch (start us, length us, event | category | flops | bytes accessed | tf_op | source)
XLA Modules:
  0.0 63.9 jit_solution(14905438099126966589)
XLA Ops:
  1.9 0.0 copy-start.2
  1.9 0.7 %copy-done.2 = s32[256]{0:T(256)S(1)} copy-done((s32[256]{0:T(256)S(1)}, s32[256]{0:T(256)}, u32[]{:S(2)}) %copy-start.2) | copy-done | bytes 1048
  2.6 0.0 copy-start
  2.6 0.8 %copy-done = f32[16,1024]{1,0:T(8,128)S(1)} copy-done((f32[16,1024]{1,0:T(8,128)S(1)}, f32[16,1024]{1,0:T(8,128)}, u32[]{:S(2)}) %copy-start) | copy-done | bytes 65560
  3.4 0.0 copy-start.1
  3.4 0.8 %copy-done.1 = f32[16,1024]{1,0:T(8,128)S(1)} copy-done((f32[16,1024]{1,0:T(8,128)S(1)}, f32[16,1024]{1,0:T(8,128)}, u32[]{:S(2)}) %copy-start.1) | copy-done | bytes 65560
  4.3 57.7 %shard_map.76 = (f32[16,1024]{1,0:T(8,128)S(1)}, f32[16,1024]{1,0:T(8,128)S(1)}, f32[8,128]{1,0:T(8,128)S(1)}) custom-call(f32[16,1024]{1,0:T(8,128)S(1)} %copy-done, f32[16,1024]{1,0:T(8,128)S(1)} %copy-done.1, s32[1,256]{1,0:T(1,128)S(1)} %bitcast.5, f32[1,1]{1,0:T(1,128)} %bitcast.3.log_scale, f32[1,1]{1,0:T(1,128)} %bitcast.4.logit_bias), custom_call_target="tpu_custom_call" | custom-call | tf_op jit(solution)/shard_map/pallas_call | solution.py:487
  62.0 0.6 slice_reduce_fusion
  62.6 0.6 copy.12
  63.3 0.6 copy.13
Async XLA Ops:
  1.9 0.7 %copy-start.2 = (s32[256]{0:T(256)S(1)}, s32[256]{0:T(256)}, u32[]{:S(2)}) copy-start(s32[256]{0:T(256)} %param.7) | copy-start | bytes 3076
  2.6 0.8 %copy-start = (f32[16,1024]{1,0:T(8,128)S(1)}, f32[16,1024]{1,0:T(8,128)}, u32[]{:S(2)}) copy-start(f32[16,1024]{1,0:T(8,128)} %segments_hbm.1) | copy-start | bytes 196612
  3.4 0.8 %copy-start.1 = (f32[16,1024]{1,0:T(8,128)S(1)}, f32[16,1024]{1,0:T(8,128)}, u32[]{:S(2)}) copy-start(f32[16,1024]{1,0:T(8,128)} %futures_hbm.1) | copy-start | bytes 196612

commit v3 on v2

--- a/solution.py
+++ b/solution.py
@@ -11,7 +11,7 @@
 epsilon = 1e-06
 
 NX, NY, NZ = 4, 4, 16
-RING = NZ // 2
+RING = 8
 ROWS = 16
 WIDTH = 1024
 CHIPS = 16
@@ -20,8 +20,8 @@
 FIRST = 10
 HALVES = 2
 HALF = ROWS // HALVES
-FAR = 4
-KZ, KX, QP, QY, QS, TG, RX, RZ, RS, RY, RP, SL, SW, SR, SY = range(15)
+FAR = 7
+KZ, KX, QP, QY, QS, TG, RX, RZ, RS, RY, RP, SG, SA = range(13)
 
 
 def coordinates():
@@ -34,14 +34,6 @@
     return (lax.rem(x, 2) * NZ + z, y * 4 + (x // 2) * 2 + core)
 
 
-def place_of(way, step):
-    return 0 if step == 0 else 7 if step == FAR else 2 * step - 1 + way
-
-
-def has(way, step, half):
-    return step < FAR or way == half
-
-
 def split(value):
     high = value.astype(bf16)
     return high, (value - high.astype(f32)).astype(bf16)
@@ -75,17 +67,18 @@
 
 def kernel(
     segments_hbm, futures_hbm, pairs_hbm, log_scale, logit_bias,
-    grad_segments, grad_futures, scalars,
-    segments, futures, pairs,
+    segments_out, futures_out, scalars_out,
+    segments, futures, pairs, grad_segments, grad_futures, scalars,
     queries, queries_high, queries_low, keys, keys_high, keys_low,
-    weights, weights_high, weights_low, key_terms, x_terms, ring_terms,
+    weights, weights_high, weights_low, key_terms, x_terms, line_terms,
     query_terms, sibling_terms, y_terms, pair_terms, z_terms, targets,
-    sums_line, sums_two, sums_row, sums_y,
-    in_sem, send, kz_recv, kx_recv, qp_recv, qy_recv, qs_recv,
+    sums_group, sums_all,
+    in_sem, out_sem, send, kz_recv, kx_recv, qp_recv, qy_recv, qs_recv,
     rx_recv, rz_recv, rs_recv, ry_recv, rp_recv, once_recv,
 ):
     x, y, z, core = coordinates()
     odd_x, odd_z = lax.rem(x, 2), lax.rem(z, 2)
+    sign = 1 - 2 * odd_z
     key_x = x + 1 - 2 * odd_x
     query_x = lax.rem(x + 2 * odd_x + NX - 1, NX)
     pair_z = z + 1 - 2 * odd_z
@@ -98,8 +91,8 @@
     def y_device(offset):
         return device(x, lax.rem(y + offset, NY), z, core)
 
-    def ring_device(steps, column=None):
-        return device(x if column is None else column, y, lax.rem(z + 2 * steps + NZ, NZ), core)
+    def line_device(distance, column=None):
+        return device(x if column is None else column, y, lax.rem(z + sign * distance + NZ, NZ), core)
 
     def row_device(offset, other):
         return device(lax.rem(x + offset, NX), y, z, 1 - core if other else core)
@@ -118,7 +111,8 @@
     barrier = pltpu.get_barrier_semaphore()
     target_peers = [z_partner, query_partner, device(query_x, y, pair_z, core)]
     row_peers = [(d, other) for d in range(NX) for other in (False, True) if d or other]
-    greeted = [ring_device(way, column) for way in (1, -1) for column in (None, key_x)] + [z_partner, target_peers[2]]
+    greeted = [line_device(d, column) for d in (2, -2) for column in (None, key_x)]
+    greeted += [line_device(-1), z_partner, target_peers[2]]
     greeted += [y_device(d) for d in range(1, NY)] + [row_device(*p) for p in row_peers]
     for other in greeted:
         pl.semaphore_signal(barrier, inc=1, device_id=other, device_id_type=MESH)
@@ -156,36 +150,33 @@
     def half_rows(half):
         return pl.ds(half * HALF, HALF)
 
-    def gather_ring(way, step, half):
+    def gather_line(place, half):
         rows = half_rows(half)
         return remote(
-            keys.at[2 * place_of(way, step - 1), rows], keys.at[2 * place_of(way, step), rows],
-            KZ, kz_recv.at[way, step - 1, half], ring_device(1 if way == 0 else -1),
-        )
-
-    def gather_far(way):
-        rows = half_rows(way)
+            keys.at[2 * max(place - 2, 0), rows], keys.at[2 * place, rows],
+            KZ, kz_recv.at[place - 1, half], line_device(-1 if place == 1 else 2),
+        )
+
+    def gather_far(half):
+        rows = half_rows(half)
         return remote(
-            keys.at[2 * place_of(way, FAR - 1), rows], keys.at[2 * RING - 1, rows],
-            KZ, kx_recv.at[RING - 1], ring_device(1 if way == 0 else -1, key_x),
+            keys.at[2 * (FAR - 2), rows], keys.at[2 * FAR + 1, rows], KZ, kx_recv.at[FAR], line_device(2, key_x)
         )
 
     def gather_x(place):
         return remote(keys.at[2 * place], keys.at[2 * place + 1], KX, kx_recv.at[place], key_partner)
 
-    def step_ring(step):
-        for half in range(HALVES):
-            for way in range(2):
-                if step > 0 and has(way, step, half):
-                    gather_ring(way, step, half).wait_recv()
-                if step < FAR and has(way, step + 1, half):
-                    gather_ring(way, step + 1, half).start()
-                    if step + 1 == FAR:
-                        gather_far(way).start()
-        if step < FAR:
-            for way in range(2):
-                if step > 0 or way == 0:
-                    gather_x(place_of(way, step)).start()
+    def step_line(*places):
+        for place in places:
+            for half in range(HALVES):
+                gather_line(place, half).wait_recv()
+                if place + 2 <= FAR:
+                    gather_line(place + 2, half).start()
+                if place + 2 == FAR:
+                    gather_far(half).start()
+        for place in places:
+            if place < FAR:
+                gather_x(place).start()
 
     def await_x(place):
         await_recv(keys.at[2 * place + 1], KX, kx_recv.at[place])
@@ -235,7 +226,10 @@
         for offset in (0, 1, 3, 2):
             split_query(query_slot(combo, offset, 1 - core))
 
-    step_ring(0)
+    for half in range(HALVES):
+        gather_line(1, half).start()
+        gather_line(2, half).start()
+    gather_x(0).start()
     gather_partner(1).start()
     gather_partner(2).start()
     spread(0)
@@ -246,14 +240,14 @@
     bias = logit_bias[...]
     spread(1)
     spread(2)
-    step_ring(1)
+    step_line(1, 2)
     take_y(0)
     spread(3)
-    step_ring(2)
+    step_line(3, 4)
     take_y(1)
     take_sibling(0)
     take_y(2)
-    step_ring(3)
+    step_line(5, 6)
     take_sibling(1)
     take_y(3)
     take_sibling(2)
@@ -268,8 +262,7 @@
         value = scale * raw + bias
         row = lax.broadcasted_iota(jnp.int32, (b - a, 1), 0) + a
         place = row // (2 * ROWS)
-        step = (place + 1) // 2
-        line = lax.rem(z + 2 * jnp.where(place % 2 == 1, RING - step, step), NZ)
+        line = lax.rem(z + NZ - sign * place, NZ)
         low_x = jnp.where(row // ROWS % 2 == 1, 1 - odd_x, odd_x)
         key_row = (low_x * NZ + line) * (ROWS * 16) + lax.axis_index("ka") * ROWS + row % ROWS
         target = jnp.concatenate([targets[i] for i in range(4)], axis=1)
@@ -294,28 +287,38 @@
         await_x(place)
     split_keys(0, FIRST)
     totals = pair_block(0, FIRST)
-    step_ring(4)
+    step_line(7)
     for place in range(FIRST // 2, RING):
         await_x(place)
     split_keys(FIRST, CHIPS)
     totals = totals + pair_block(FIRST, CHIPS)
+
+    def start_group():
+        place = column(0) * 8 + y * 2 + core
+        sums_group[place] = totals
+        slot = sums_group.at[place]
+        for i in range(1, 2 * CHIPS):
+            far_x, far_z = query_x if i // 8 % 2 else x, pair_z if i // 16 else z
+            to = device(far_x, lax.rem(y + i // 2, NY), far_z, lax.rem(core + i, 2))
+            remote(slot, slot, SG, once_recv.at[1], to).start()
+
+    start_group()
     key_block(FIRST, CHIPS)
 
     def sum_x(place):
         return remote(key_terms.at[2 * place + 1], x_terms.at[place], RX, rx_recv.at[place], key_partner)
 
-    def sum_far(way):
-        rows = half_rows(way)
-        return remote(
-            key_terms.at[2 * RING - 1, rows], x_terms.at[RING - 1, rows],
-            RX, rx_recv.at[RING - 1 + way], ring_device(-1 if way == 0 else 1, key_x),
-        )
-
-    def sum_ring(way, step, half):
+    def sum_far(half):
         rows = half_rows(half)
         return remote(
-            key_terms.at[2 * place_of(way, step), rows], ring_terms.at[way, step - 1, rows],
-            RZ, rz_recv.at[way, step - 1, half], ring_device(-1 if way == 0 else 1),
+            key_terms.at[2 * FAR + 1, rows], x_terms.at[FAR, rows], RX, rx_recv.at[FAR + half], line_device(-2, key_x)
+        )
+
+    def sum_line(place, half):
+        rows = half_rows(half)
+        return remote(
+            key_terms.at[2 * place, rows], line_terms.at[place - 1, rows],
+            RZ, rz_recv.at[place - 1, half], line_device(-1 if place == 1 else -2),
         )
 
     def start_x(*places):
@@ -323,60 +326,42 @@
             sum_x(place).start()
 
     def start_far():
-        for way in range(2):
-            sum_ring(way, FAR, way).start()
-            sum_far(way).start()
-
-    def reduce_ring(step):
+        for half in range(HALVES):
+            sum_line(FAR, half).start()
+            sum_far(half).start()
+
+    def reduce_line(place):
+        sum_x(place).wait_recv()
         for half in range(HALVES):
             rows = half_rows(half)
-            for way in range(2):
-                place = place_of(way, step)
-                if half == 0:
-                    sum_x(place).wait_recv()
-                total = key_terms[2 * place, rows] + x_terms[place, rows]
-                if has(way, step + 1, half):
-                    sum_ring(way, step + 1, half).wait_recv()
-                    total = total + ring_terms[way, step, rows]
-                if step + 1 == FAR and way == half:
-                    sum_far(way).wait_recv()
-                    total = total + x_terms[RING - 1, rows]
-                key_terms[2 * place, rows] = total
-                sum_ring(way, step, half).start()
+            total = key_terms[2 * place, rows] + x_terms[place, rows]
+            if place + 2 <= FAR:
+                sum_line(place + 2, half).wait_recv()
+                total = total + line_terms[place + 1, rows]
+            if place + 2 == FAR:
+                sum_far(half).wait_recv()
+                total = total + x_terms[FAR, rows]
+            key_terms[2 * place, rows] = total
+            sum_line(place, half).start()
 
     start_far()
     start_x(5, 6)
 
-    def start_line():
-        slot = sums_line.at[z // 2]
-        sums_line[z // 2] = totals
-        for d in range(1, RING):
-            remote(slot, slot, SL, once_recv.at[1], ring_device(d)).start()
-
-    def start_two():
-        await_recv(sums_line.at[pl.ds(0, RING - 1)], SL, once_recv.at[1])
-        sums_two[odd_z] = jnp.sum(sums_line[...], axis=0)
-        slot = sums_two.at[odd_z]
-        remote(slot, slot, SW, once_recv.at[2], z_partner).start()
-
-    def start_row():
-        await_recv(sums_two.at[0], SW, once_recv.at[2])
-        sums_row[x * 2 + core] = sums_two[0] + sums_two[1]
-        slot = sums_row.at[x * 2 + core]
-        for p in row_peers:
-            remote(slot, slot, SR, once_recv.at[3], row_device(*p)).start()
-
-    def start_column():
-        await_recv(sums_row.at[pl.ds(0, 2 * NX - 1)], SR, once_recv.at[3])
-        sums_y[y] = jnp.sum(sums_row[...], axis=0)
-        slot = sums_y.at[y]
-        for d in range(1, NY):
-            remote(slot, slot, SY, once_recv.at[4], y_device(d)).start()
+    def start_all():
+        await_recv(sums_group.at[pl.ds(0, 2 * CHIPS - 1)], SG, once_recv.at[1])
+        place = z // 2 * 2 + lax.rem((x + 1) // 2, 2)
+        sums_all[place] = jnp.sum(sums_group[...], axis=0)
+        slot = sums_all.at[place]
+        for d in range(RING):
+            if d > 0:
+                remote(slot, slot, SA, once_recv.at[2], line_device(-d)).start()
+            remote(slot, slot, SA, once_recv.at[2], line_device(-d, key_x)).start()
 
     def finish_scalars():
-        await_recv(sums_y.at[pl.ds(0, NY - 1)], SY, once_recv.at[4])
-        total = jnp.sum(sums_y[...], axis=0) * f32(1.0 / 8192)
-        scalars[...] = jnp.broadcast_to(jnp.sum(total, axis=1, keepdims=True), scalars.shape)
+        await_recv(sums_all.at[pl.ds(0, CHIPS - 1)], SA, once_recv.at[2])
+        total = jnp.sum(sums_all[...], axis=0) * f32(1.0 / 8192)
+        for i in range(3):
+            scalars[i] = jnp.sum(total[i : i + 1, :])
 
     def query_block(combo):
         rows = pl.ds(pl.multiple_of(column(combo) * 8 * ROWS, 8 * ROWS), 8 * ROWS)
@@ -412,7 +397,6 @@
             z_partner if combo == 1 else query_partner,
         )
 
-    start_line()
     high, low = split(weights[...].T)
     weights_high[...] = high
     weights_low[...] = low
@@ -423,22 +407,23 @@
     start_y(2)
     query_block(0)
     start_y(1)
-    reduce_ring(3)
+    reduce_line(6)
+    reduce_line(5)
     key_block(0, FIRST)
     start_x(3, 4, 1, 2, 0)
     start_y(0)
-    start_two()
-    reduce_ring(2)
+    start_all()
+    reduce_line(3)
+    reduce_line(4)
     for combo in (3, 2):
         pair_terms[combo] = take_column(combo)
         sum_partner(combo).start()
-    start_row()
     near = take_column(1)
     sum_partner(3).wait_recv()
     pair_terms[1] = near + z_terms[3]
     sum_partner(1).start()
-    reduce_ring(1)
-    start_column()
+    reduce_line(1)
+    reduce_line(2)
 
     query_grad = take_column(0)
     sum_partner(2).wait_recv()
@@ -446,15 +431,23 @@
     sum_partner(1).wait_recv()
     query_grad = query_grad + z_terms[1]
     grad_segments[...] = backward(query_unit, query_grad, query_inverse)
+    stores = [
+        pltpu.make_async_copy(grad_segments, segments_out, out_sem.at[0]),
+        pltpu.make_async_copy(scalars, scalars_out, out_sem.at[1]),
+        pltpu.make_async_copy(grad_futures, futures_out, out_sem.at[2]),
+    ]
+    stores[0].start()
 
     finish_scalars()
+    stores[1].start()
 
     sum_x(0).wait_recv()
     for half in range(HALVES):
-        for way in range(2):
-            sum_ring(way, 1, half).wait_recv()
-    key_grad = (key_terms[0] + x_terms[0]) + (ring_terms[0, 0] + ring_terms[1, 0])
+        sum_line(1, half).wait_recv()
+        sum_line(2, half).wait_recv()
+    key_grad = (key_terms[0] + x_terms[0]) + (line_terms[0] + line_terms[1])
     grad_futures[...] = backward(key_unit, key_grad, key_inverse)
+    stores[2].start()
 
     def blocks(ref, count):
         return ref.at[pl.ds(0, count)]
@@ -470,10 +463,10 @@
     await_send(blocks(queries, 16), RS)
     await_send(blocks(queries, 12), RY)
     await_send(blocks(queries, 3), RP)
-    await_send(blocks(sums_line, RING - 1), SL)
-    await_send(sums_two.at[0], SW)
-    await_send(blocks(sums_row, 2 * NX - 1), SR)
-    await_send(blocks(sums_y, NY - 1), SY)
+    await_send(blocks(sums_group, 2 * CHIPS - 1), SG)
+    await_send(blocks(sums_all, CHIPS - 1), SA)
+    for store in stores:
+        store.wait()
 
 
 def per_device(segments, futures, pair_index, log_scale, logit_bias):
@@ -489,14 +482,17 @@
         out_shape=(
             jax.ShapeDtypeStruct(block, f32),
             jax.ShapeDtypeStruct(block, f32),
-            jax.ShapeDtypeStruct(sums, f32),
+            jax.ShapeDtypeStruct((3,), f32),
         ),
         in_specs=[in_hbm] * 3 + [in_vmem] * 2,
-        out_specs=(in_vmem, in_vmem, in_vmem),
+        out_specs=(in_hbm,) * 3,
         scratch_shapes=[
             vmem(block, f32),
             vmem(block, f32),
             vmem((1, 256), jnp.int32),
+            vmem(block, f32),
+            vmem(block, f32),
+            pltpu.SMEM((3,), f32),
             vmem((CHIPS * 2,) + block, f32),
             vmem((QUERIES, WIDTH), bf16),
             vmem((QUERIES, WIDTH), bf16),
@@ -508,33 +504,32 @@
             vmem((QUERIES, KEYS), bf16),
             vmem((CHIPS,) + block, f32),
             vmem((RING,) + block, f32),
-            vmem((2, FAR) + block, f32),
+            vmem((FAR,) + block, f32),
             vmem((4, NY, 2) + block, f32),
             vmem((4, NY) + block, f32),
             vmem((4, NY) + block, f32),
             vmem((4,) + block, f32),
             vmem((4,) + block, f32),
             vmem((4, 1, 128), jnp.int32),
-            vmem((RING,) + sums, f32),
-            vmem((2,) + sums, f32),
-            vmem((2 * NX,) + sums, f32),
-            vmem((NY,) + sums, f32),
+            vmem((2 * CHIPS,) + sums, f32),
+            vmem((CHIPS,) + sums, f32),
             dma((3,)),
-            dma((15,)),
-            dma((2, FAR, HALVES)),
+            dma((3,)),
+            dma((13,)),
+            dma((FAR, HALVES)),
             dma((RING,)),
             dma((4,)),
             dma((4,)),
             dma((4,)),
             dma((RING + 1,)),
-            dma((2, FAR, HALVES)),
+            dma((FAR, HALVES)),
             dma((4,)),
             dma((4,)),
             dma((4,)),
-            dma((5,)),
+            dma((3,)),
         ],
         compiler_params=pltpu.CompilerParams(
-            collective_id=0, has_side_effects=True, vmem_limit_bytes=40 << 20
+            collective_id=0, has_side_effects=True, vmem_limit_bytes=62 << 20
         ),
     )(
         segments,
@@ -543,7 +538,7 @@
         log_scale.reshape(1, 1),
         logit_bias.reshape(1, 1),
     )
-    return grad_segments, grad_futures, scalars[:3, 0]
+    return grad_segments, grad_futures, scalars
 
 
 def solution(mesh):

time: 64.1 us -> 61 us (0.952)
  the two profiles are of different devices: /device:TPU:3 before, /device:TPU:34 now
where the time goes in v3:
time: 61 us; the launch traced here: 60.8 us
  Pallas kernels  56.2 us (92%)
  local copies, waits for them, and re-layouts  2.65 us (4%)
  between operations  1.94 us (3%)
    pallas_call x1, Pallas kernels, per_device(): pl.pallas_call(kernel, out_shape=(jax.ShapeDtypeStruct(block, f32), jax.S...  56.2 us
    unnamed x7, local copies, waits for them, and re-layouts  2.65 us

profile of v3, /device:TPU:34, one launch (start us, length us, event | category | flops | bytes accessed | tf_op | source)
XLA Modules:
  0.0 60.8 jit_solution(4732159708912847729)
XLA Ops:
  1.9 56.2 %shard_map.76 = (f32[16,1024]{1,0:T(8,128)}, f32[16,1024]{1,0:T(8,128)}, f32[3]{0:T(128)}) custom-call(f32[16,1024]{1,0:T(8,128)} %segments_hbm.1, f32[16,1024]{1,0:T(8,128)} %futures_hbm.1, s32[1,256]{1,0:T(1,128)} %bitcast.5, f32[1,1]{1,0:T(1,128)} %bitcast.3.log_scale, f32[1,1]{1,0:T(1,128)} %bitcast.4.logit_bias), custom_call_target="tpu_custom_call" | custom-call | tf_op jit(solution)/shard_map/pallas_call | solution.py:480
  58.1 0.0 copy-start
  58.1 1.5 %copy.13 = f32[16,1024]{1,0:T(8,128)} copy(f32[16,1024]{1,0:T(8,128)} %get-tuple-element.6) | data formatting | bytes 131072
  59.6 0.0 copy-done
  59.6 0.0 copy-start.1
  59.6 0.6 %copy.14 = f32[16,1024]{1,0:T(8,128)} copy(f32[16,1024]{1,0:T(8,128)S(1)} %copy-done) | data formatting | bytes 131072
  60.3 0.0 copy-done.1
  60.3 0.5 copy.15
Async XLA Ops:
  58.1 1.5 %copy-start = (f32[16,1024]{1,0:T(8,128)S(1)}, f32[16,1024]{1,0:T(8,128)}, u32[]{:S(2)}) copy-start(f32[16,1024]{1,0:T(8,128)} %get-tuple-element.7) | copy-start | bytes 196612
  59.6 0.6 %copy-start.1 = (f32[3]{0:T(128)S(1)}, f32[3]{0:T(128)}, u32[]{:S(2)}) copy-start(f32[3]{0:T(128)} %get-tuple-element.8) | copy-start | bytes 40

commit v4 on v3

--- a/solution.py
+++ b/solution.py
@@ -238,9 +238,9 @@
         remote(mine_target, mine_target, TG, once_recv.at[0], to).start()
     scale = jnp.exp(log_scale[...])
     bias = logit_bias[...]
+    step_line(1, 2)
     spread(1)
     spread(2)
-    step_line(1, 2)
     take_y(0)
     spread(3)
     step_line(3, 4)
@@ -529,7 +529,7 @@
             dma((3,)),
         ],
         compiler_params=pltpu.CompilerParams(
-            collective_id=0, has_side_effects=True, vmem_limit_bytes=62 << 20
+            collective_id=0, has_side_effects=True, vmem_limit_bytes=55060 << 10
         ),
     )(
         segments,

time: 61 us -> 59.8 us (0.980)
  the two profiles are of different devices: /device:TPU:34 before, /device:TPU:38 now
where the time goes in v4:
time: 59.8 us; the launch traced here: 59.6 us
  Pallas kernels  55.2 us (92%)
  local copies, waits for them, and re-layouts  2.44 us (4%)
  between operations  1.94 us (3%)
    pallas_call x1, Pallas kernels, per_device(): pl.pallas_call(kernel, out_shape=(jax.ShapeDtypeStruct(block, f32), jax.S...  55.2 us
    unnamed x5, local copies, waits for them, and re-layouts  2.44 us

profile of v4, /device:TPU:38, one launch (start us, length us, event | category | flops | bytes accessed | tf_op | source)
XLA Modules:
  0.0 59.6 jit_solution(13917731999932037447)
XLA Ops:
  1.9 0.0 copy-start
  1.9 0.7 %copy-done = s32[256]{0:T(256)S(1)} copy-done((s32[256]{0:T(256)S(1)}, s32[256]{0:T(256)}, u32[]{:S(2)}) %copy-start) | copy-done | bytes 1048
  2.6 55.2 %shard_map.76 = (f32[16,1024]{1,0:T(8,128)S(1)}, f32[16,1024]{1,0:T(8,128)S(1)}, f32[3]{0:T(128)S(1)}) custom-call(f32[16,1024]{1,0:T(8,128)} %segments_hbm.1, f32[16,1024]{1,0:T(8,128)} %futures_hbm.1, s32[1,256]{1,0:T(1,128)S(1)} %bitcast.5, f32[1,1]{1,0:T(1,128)} %bitcast.3.log_scale, f32[1,1]{1,0:T(1,128)} %bitcast.4.logit_bias), custom_call_target="tpu_custom_call" | custom-call | tf_op jit(solution)/shard_map/pallas_call | solution.py:480
  57.8 0.6 %copy.13 = f32[16,1024]{1,0:T(8,128)} copy(f32[16,1024]{1,0:T(8,128)S(1)} %get-tuple-element.6) | data formatting | bytes 131072
  58.4 0.6 %copy.14 = f32[16,1024]{1,0:T(8,128)} copy(f32[16,1024]{1,0:T(8,128)S(1)} %get-tuple-element.7) | data formatting | bytes 131072
  59.1 0.5 copy.15
Async XLA Ops:
  1.9 0.7 %copy-start = (s32[256]{0:T(256)S(1)}, s32[256]{0:T(256)}, u32[]{:S(2)}) copy-start(s32[256]{0:T(256)} %param.7) | copy-start | bytes 3076
